TPU v7x, 512 devices: a whole 4x4x16 slice. The times are simulated.
512 devices in a mesh: blk: 16 (over z), tp: 32 (over y, x, core).
Axes of the slice: x: 4, y: 4, z: 16, core: 2. Of those that a mesh axis runs over, the one named last changes fastest.
Arguments:
- weights: float32 [16, 28672, 384], P('blk', 'tp'), may hold values from -71 to 71
- hidden: bfloat16 [16384, 28672], P('blk', 'tp'), may hold values from -6 to 6
- grad_out: bfloat16 [16384, 384], P('blk'), may hold values from -6 to 6
- warm_start: float32 [16, 8, 384], replicated, may hold values from -6 to 6
Outputs:
- new_weights: float32 [16, 28672, 384], P('blk', 'tp')
- next_start: float32 [16, 8, 384], P('blk')
All inputs are finite; a program needn't handle non-finite values.
Results may differ from a plain program's by a relative error of at most 0.0003.
Values sent between devices are 32-bit elements; how exact they have to be, the bound alone decides.
A program may use at most 64 MiB of HBM per device.

v0:
```python
import math

import jax
import jax.numpy as jnp
from jax import lax
from jax.sharding import PartitionSpec as P

step_rate = 0.5
mix_rate = 0.5


def padded_2(cells, sides, width):
    for axis, dim in sides:
        count = lax.axis_size(axis)
        head = lax.slice_in_dim(cells, 0, width, axis=dim)
        tail = lax.slice_in_dim(cells, cells.shape[dim] - width, cells.shape[dim], axis=dim)
        cells = jnp.concatenate(
            [
                lax.ppermute(tail, axis, [(i, (i + 1) % count) for i in range(count)]),
                cells,
                lax.ppermute(head, axis, [((i + 1) % count, i) for i in range(count)]),
            ],
            axis=dim,
        )
    return cells


def forward_solve(lower_factor, rows):
    solved = []
    for column in range(lower_factor.shape[-1]):
        running = rows[..., column, :]
        for earlier in range(column):
            running = running - lower_factor[..., column, earlier][..., None] * solved[earlier]
        solved.append(running / lower_factor[..., column, column][..., None])
    return jnp.stack(solved, axis=-2)


def edge_pairs(padded):
    return jnp.stack([padded[0] - padded[1], padded[2] - padded[3]])


def local(weights, hidden, grad_out, warm_start):
    highest = lax.Precision.HIGHEST
    cycle_size = lax.axis_size("blk")
    position = lax.axis_index("blk")
    factor = step_rate / math.sqrt(hidden.shape[0])
    own_start = lax.dynamic_index_in_dim(warm_start, position, 0, keepdims=False)
    left_index = (position + cycle_size - 1) % cycle_size
    left_start = lax.dynamic_index_in_dim(warm_start, left_index, 0, keepdims=False)
    starts = jnp.stack([left_start, own_start])
    master = weights[0]
    gradient = lax.dot_general(
        hidden, grad_out, (((0,), (0,)), ((), ())), preferred_element_type=jnp.float32
    )
    stepped = master - factor * gradient
    own_images = jnp.einsum("fs,ers->erf", stepped, starts, precision=highest)
    padded = padded_2(own_images, (("blk", 0),), 1)
    images = edge_pairs(padded)
    partial_gram = jnp.einsum("erf,esf->ers", images, images, precision=highest)
    gram_matrix = lax.psum(partial_gram, "tp")
    lower_factor = jnp.linalg.cholesky(gram_matrix)
    basis_rows = forward_solve(lower_factor, images)
    partial_back = jnp.einsum("erf,fs->ers", basis_rows, stepped, precision=highest)
    back_products = lax.psum(partial_back, "tp")
    neighbours = padded_2(back_products, (("blk", 0),), 1)
    following = edge_pairs(neighbours)
    correction = jnp.einsum("rf,rs->fs", basis_rows[1], following[1], precision=highest)
    correction = correction - jnp.einsum(
        "rf,rs->fs", basis_rows[0], following[0], precision=highest
    )
    new_weights = stepped - mix_rate * correction
    return (new_weights[None], following[1][None])


def solution(mesh):
    return jax.shard_map(
        local,
        mesh=mesh,
        in_specs=(P("blk", "tp", None), P("blk", "tp"), P("blk", None), P()),
        out_specs=(P("blk", "tp", None), P("blk", None, None)),
        check_vma=False,
    )
```

profile of v0, /device:TPU:1, one launch (start us, length us, event | category | flops | bytes accessed | tf_op | source)
XLA Modules:
  0.0 230.4 jit_solution(12539008276878927804)
XLA Ops:
  0.6 0.0 copy-start
  0.7 0.9 constant_dynamic-slice_fusion.1
  1.5 0.6 copy-done
  2.2 2.7 %fusion.3 = f32[896,384]{1,0:T(8,128)S(1)} fusion(bf16[1024,896]{1,0:T(8,128)(2,1)S(1)} %copy-done, bf16[1024,384]{1,0:T(8,128)(2,1)} %param.6, f32[1,896,384]{2,1,0:T(8,128)} %param.4), kind=kOutput, calls=%fused_computation.5 | convolution fusion | flops 705331200 | bytes 5373952 | tf_op jit(solution)/shard_map/dot_general | solution.py:52
  4.9 1.3 fusion.6
  6.2 4.4 %collective-permute-start = (f32[1,8,896]{2,0,1:T(1,128)S(1)}, f32[1,8,896]{2,0,1:T(1,128)S(1)}, u32[]{:S(2)}, u32[]{:S(2)}) collective-permute-start(f32[1,8,896]{2,0,1:T(1,128)S(1)} %copy.22), channel_id=1, source_target_pairs={{0,32},{32,64},{64,96},{96,128},{128,160},{160,192},{192,224},{224... | collective-permute-start | bytes 86024 | tf_op jit(solution)/shard_map/ppermute | solution.py:19
  10.6 8.8 %collective-permute-done = f32[1,8,896]{2,0,1:T(1,128)S(1)} collective-permute-done((f32[1,8,896]{2,0,1:T(1,128)S(1)}, f32[1,8,896]{2,0,1:T(1,128)S(1)}, u32[]{:S(2)}, u32[]{:S(2)}) %collective-permute-start) | collective-permute-done | bytes 28704 | tf_op jit(solution)/shard_map/ppermute | solution.py:19
  19.4 0.1 copy_subtract_fusion
  19.5 3.4 %collective-permute-start.1 = (f32[1,8,896]{2,0,1:T(1,128)S(1)}, f32[1,8,896]{2,0,1:T(1,128)S(1)}, u32[]{:S(2)}, u32[]{:S(2)}) collective-permute-start(f32[1,8,896]{2,0,1:T(1,128)S(1)} %get-tuple-element.59), channel_id=1, source_target_pairs={{32,0},{64,32},{96,64},{128,96},{160,128},{192,160},{224,192},{256... | collective-permute-start | bytes 86024 | tf_op jit(solution)/shard_map/ppermute | solution.py:21
  22.9 1.2 collective-permute-done.1
  24.1 0.1 pad_maximum_fusion
  24.2 0.2 fusion.9
  24.4 66.0 %psum.14 = f32[2,8,8]{1,2,0:T(8,128)S(1)} all-reduce(f32[2,8,8]{1,2,0:T(8,128)S(1)} %fusion.9), channel_id=1, replica_groups=mesh['blk'=16,'tp'=32] {'tp'}, use_global_device_ids=true, to_apply=%region_0.1 | all-reduce | flops 128 | bytes 1024 | tf_op jit(solution)/shard_map/psum | solution.py:60
  90.4 0.1 copy.17
  90.5 1.4 custom-call.4
  91.9 0.1 select_reduce_fusion
  92.0 0.1 compare_reduce_fusion
  92.1 0.1 select_select_fusion
  92.2 0.2 slice_reduce_fusion.20
  92.4 0.2 slice_reduce_fusion.7
  92.6 0.1 constant_dynamic-update-slice_fusion.7
  92.7 0.1 constant_dynamic-update-slice_fusion.6
  92.8 0.1 constant_dynamic-update-slice_fusion.5
  92.8 0.1 constant_dynamic-update-slice_fusion.4
  92.9 0.1 constant_dynamic-update-slice_fusion.3
  93.0 0.1 constant_dynamic-update-slice_fusion.2
  93.1 0.1 constant_dynamic-update-slice_fusion.1
  93.2 0.1 constant_dynamic-update-slice_fusion
  93.3 0.8 fusion.4
  94.1 121.2 %psum.15 = f32[2,8,384]{2,1,0:T(8,128)S(1)} all-reduce(f32[2,8,384]{2,1,0:T(8,128)S(1)} %fusion.4), channel_id=1, replica_groups=mesh['blk'=16,'tp'=32] {'tp'}, use_global_device_ids=true, to_apply=%region_3.4 | all-reduce | flops 6144 | bytes 49152 | tf_op jit(solution)/shard_map/psum | solution.py:64
  215.3 4.6 %collective-permute-start.2 = (f32[1,8,384]{2,1,0:T(8,128)S(1)}, f32[1,8,384]{2,1,0:T(8,128)S(1)}, u32[]{:S(2)}, u32[]{:S(2)}) collective-permute-start(f32[1,8,384]{2,1,0:T(8,128)S(1)} %slice.266), channel_id=1, source_target_pairs={{32,0},{64,32},{96,64},{128,96},{160,128},{192,160},{224,192},{256... | collective-permute-start | bytes 36872 | tf_op jit(solution)/shard_map/ppermute | solution.py:21
  219.8 0.8 collective-permute-done.2
  220.6 0.0 copy-start.1
  220.6 1.9 collective-permute-start.3
  222.6 3.9 %collective-permute-done.3 = f32[1,8,384]{2,1,0:T(8,128)S(1)} collective-permute-done((f32[1,8,384]{2,1,0:T(8,128)S(1)}, f32[1,8,384]{2,1,0:T(8,128)S(1)}, u32[]{:S(2)}, u32[]{:S(2)}) %collective-permute-start.3) | collective-permute-done | bytes 12320 | tf_op jit(solution)/shard_map/ppermute | solution.py:19
  226.5 1.3 fusion.11
  227.9 2.5 %fusion.2 = f32[1,896,384]{2,1,0:T(8,128)} fusion(f32[896,384]{1,0:T(8,128)S(1)} %fusion.3, f32[896,384]{1,0:T(8,128)S(1)} %fusion.11, f32[1,8,896]{2,0,1:T(1,128)S(1)} %get-tuple-element.54, f32[1,8,384]{2,1,0:T(8,128)S(1)} %get-tuple-element.60), kind=kOutput, calls=%fused_computation.3 | convolution fusion | flops 34062336 | bytes 4169728 | tf_op jit(solution)/shard_map/rf,rs->fs/dot_general | solution.py:67
  230.4 0.0 copy-done.1
  (9 shorter events, 0.2 us)
Async XLA Ops:
  0.6 1.5 copy-start
  6.2 13.2 %collective-permute-start = (f32[1,8,896]{2,0,1:T(1,128)S(1)}, f32[1,8,896]{2,0,1:T(1,128)S(1)}, u32[]{:S(2)}, u32[]{:S(2)}) collective-permute-start(f32[1,8,896]{2,0,1:T(1,128)S(1)} %copy.22), channel_id=1, source_target_pairs={{0,32},{32,64},{64,96},{96,128},{128,160},{160,192},{192,224},{224... | collective-permute-start | bytes 86024 | tf_op jit(solution)/shard_map/ppermute | solution.py:19
  19.5 4.6 %collective-permute-start.1 = (f32[1,8,896]{2,0,1:T(1,128)S(1)}, f32[1,8,896]{2,0,1:T(1,128)S(1)}, u32[]{:S(2)}, u32[]{:S(2)}) collective-permute-start(f32[1,8,896]{2,0,1:T(1,128)S(1)} %get-tuple-element.59), channel_id=1, source_target_pairs={{32,0},{64,32},{96,64},{128,96},{160,128},{192,160},{224,192},{256... | collective-permute-start | bytes 86024 | tf_op jit(solution)/shard_map/ppermute | solution.py:21
  215.3 5.4 %collective-permute-start.2 = (f32[1,8,384]{2,1,0:T(8,128)S(1)}, f32[1,8,384]{2,1,0:T(8,128)S(1)}, u32[]{:S(2)}, u32[]{:S(2)}) collective-permute-start(f32[1,8,384]{2,1,0:T(8,128)S(1)} %slice.266), channel_id=1, source_target_pairs={{32,0},{64,32},{96,64},{128,96},{160,128},{192,160},{224,192},{256... | collective-permute-start | bytes 36872 | tf_op jit(solution)/shard_map/ppermute | solution.py:21
  220.6 9.8 %copy-start.1 = (f32[1,8,384]{2,1,0:T(8,128)}, f32[1,8,384]{2,1,0:T(8,128)S(1)}, u32[]{:S(2)}) copy-start(f32[1,8,384]{2,1,0:T(8,128)S(1)} %get-tuple-element.60) | copy-start | bytes 36868
  220.6 5.9 %collective-permute-start.3 = (f32[1,8,384]{2,1,0:T(8,128)S(1)}, f32[1,8,384]{2,1,0:T(8,128)S(1)}, u32[]{:S(2)}, u32[]{:S(2)}) collective-permute-start(f32[1,8,384]{2,1,0:T(8,128)S(1)} %get-tuple-element.61), channel_id=1, source_target_pairs={{0,32},{32,64},{64,96},{96,128},{128,160},{160,192},{192,224},{224... | collective-permute-start | bytes 36872 | tf_op jit(solution)/shard_map/ppermute | solution.py:19
where the time goes:
time: 234 us; the launch traced here: 230 us
  blocking collectives  187 us (80%)
  waiting for transfers between devices  14.8 us (6%)
  starting transfers between devices  14.2 us (6%)
  matrix products  8.83 us (4%)
  other arithmetic  2.57 us (1%)
    psum x1, blocking collectives, local(): back_products = lax.psum(partial_back, 'tp')  121 us
    psum x1, blocking collectives, local(): gram_matrix = lax.psum(partial_gram, 'tp')  66 us
    ppermute x2, waiting for transfers between devices, padded_2(): lax.ppermute(tail, axis, [(i, (i + 1) % count) for i in range(count)])  12.7 us
    ppermute x2, starting transfers between devices, padded_2(): lax.ppermute(head, axis, [((i + 1) % count, i) for i in range(count)])  7.92 us
    ppermute x2, starting transfers between devices, padded_2(): lax.ppermute(tail, axis, [(i, (i + 1) % count) for i in range(count)])  6.29 us
  transfers between devices with their start and end apart: 4, of which 4 were waited for; matrix products, arithmetic and copies ran while one was open for 0% of the time, Pallas kernels for 0%

commit v1 on v0

v1 whole, which is shorter than its diff:
```python
import functools
import math

import jax
import jax.numpy as jnp
from jax import lax
from jax.experimental import pallas as pl
from jax.experimental.pallas import tpu as pltpu
from jax.sharding import PartitionSpec as P

step_rate = 0.5
mix_rate = 0.5
MESH = pl.DeviceIdType.MESH
X, Y, C = 4, 4, 2
RANK = 8
PIECES = 14
F32, BF16 = jnp.float32, jnp.bfloat16


def split3(v):
    high = v.astype(BF16)
    rest = v - high.astype(F32)
    mid = rest.astype(BF16)
    low = (rest - mid.astype(F32)).astype(BF16)
    return high, mid, low


def dot(a, b, dims):
    return lax.dot_general(a, b, (dims, ((), ())), preferred_element_type=F32)


def six_pass(rows, stacks, dims):
    n = rows[0].shape[0]
    high, mid, low = stacks
    a = dot(jnp.concatenate(rows, axis=0), high, dims)
    b = dot(jnp.concatenate(rows[:2], axis=0), mid, dims)
    c = dot(rows[0], low, dims)
    small = a[2 * n :] + b[n:] + c
    return a[:n] + (a[n : 2 * n] + b[:n] + small)


def send(src, dst, send_sem, recv_sem, peer):
    copy = pltpu.make_async_remote_copy(
        src_ref=src, dst_ref=dst, send_sem=send_sem, recv_sem=recv_sem,
        device_id=peer, device_id_type=MESH,
    )
    copy.start()
    return copy


def kernel(
    count, chunks, factor,
    w_hbm, h_hbm, g_hbm, s_hbm, *rest,
):
    steps, images, rest = rest[:PIECES], rest[PIECES : 2 * PIECES], rest[2 * PIECES :]
    mix_ref, next_ref, w_v, h_v, g_v, start_v, parts_v, own, land, part = rest[:10]
    zbuf, zsum, xbuf, xsum, ybuf, load_sems = rest[10:16]
    isend, irecv, zsend, zrecv, xsend, xrecv, ysend, yrecv = rest[16:]
    tall_rows = steps[0].shape[0]
    r = lax.axis_index("blk")
    t = lax.axis_index("tp")
    core = lax.rem(t, C)
    x = lax.rem(lax.div(t, C), X)
    y = lax.div(t, C * X)
    right = lax.rem(r + 1, count)
    left = lax.rem(r + count - 1, count)
    chip = t - core
    slab = w_v.shape[1]

    def at(yy, xx, cc):
        return (yy * X + xx) * C + cc

    loads = [
        pltpu.make_async_copy(s_hbm.at[r], start_v.at[0], load_sems.at[1]),
        pltpu.make_async_copy(s_hbm.at[left], start_v.at[1], load_sems.at[2]),
        pltpu.make_async_copy(g_hbm, g_v, load_sems.at[0]),
    ]
    for copy in loads:
        copy.start()
    chunk_loads = []
    for i, (lo, size) in enumerate(chunks):
        w_copy = pltpu.make_async_copy(
            w_hbm.at[pl.ds(lo, size)], w_v.at[pl.ds(lo, size)], load_sems.at[4 + 2 * i]
        )
        h_copy = pltpu.make_async_copy(
            h_hbm.at[:, pl.ds(lo, size)], h_v.at[:, pl.ds(lo, size)], load_sems.at[3 + 2 * i]
        )
        w_copy.start()
        h_copy.start()
        chunk_loads.append((w_copy, h_copy))

    barrier = pltpu.get_barrier_semaphore()
    peers = [(right, chip), (right, chip + 1), (left, chip), (left, chip + 1), (r, chip + 1 - core)]
    for k in range(1, X):
        peers.append((r, at(y, lax.rem(x + k, X), core)))
    for k in range(1, Y):
        for cc in range(C):
            peers.append((r, at(lax.rem(y + k, Y), x, cc)))
    for peer in peers:
        pl.semaphore_signal(barrier, inc=1, device_id=peer, device_id_type=MESH)

    part[...] = jnp.zeros_like(part)
    for copy in loads:
        copy.wait()
    starts = start_v[...].reshape(2 * RANK, slab)
    start_parts = split3(starts)
    tall = jnp.concatenate(start_parts, axis=0)
    n = 2 * RANK
    felt = dot(tall, g_v[...], ((1,), (1,)))
    felt = factor * (felt[:n] + (felt[n : 2 * n] + felt[2 * n :]))
    felt_tall = jnp.concatenate(split3(felt), axis=0)

    image_copies = []
    for i, (lo, size) in enumerate(chunks):
        span = pl.ds(lo, size)
        chunk_loads[i][0].wait()
        image = six_pass(start_parts, split3(w_v[span, :]), ((1,), (1,)))
        chunk_loads[i][1].wait()
        pulled = dot(felt_tall, h_v[:, span], ((1,), (0,)))
        image = image - (pulled[:n] + (pulled[n : 2 * n] + pulled[2 * n :]))
        own[0, :, span] = image[:RANK]
        own[1, :, span] = image[RANK:]
        if i == 0:
            pl.semaphore_wait(barrier, len(peers))
        image_copies.append(
            (
                send(own.at[0, :, span], land.at[1, :, span], isend.at[2 * i], irecv.at[2 * i], (right, t)),
                send(own.at[1, :, span], land.at[0, :, span], isend.at[2 * i + 1], irecv.at[2 * i + 1], (left, t)),
            )
        )

    for lo, size in chunks:
        span = pl.ds(lo, size)
        gradient = dot(h_v[:, span], g_v[...], ((0,), (0,)))
        stepped = w_v[span, :] - factor * gradient
        for p in range(lo // tall_rows, (lo + size) // tall_rows):
            steps[p][...] = stepped[p * tall_rows - lo : (p + 1) * tall_rows - lo]
        stacks = split3(stepped)
        for k in range(3):
            parts_v[k, span, :] = stacks[k]

    product = jnp.zeros((n, slab), F32)
    gram = jnp.zeros((n, n), F32)
    saved = []
    for i, (lo, size) in enumerate(chunks):
        span = pl.ds(lo, size)
        for copy in image_copies[i]:
            copy.wait_recv()
        edge = [own[0, :, span] - land[0, :, span], land[1, :, span] - own[1, :, span]]
        pieces = split3(jnp.concatenate(edge, axis=0))
        product = product + six_pass(pieces, [parts_v[k, span, :] for k in range(3)], ((1,), (0,)))
        gram = gram + six_pass(pieces, pieces, ((1,), (1,)))
        saved.append(pieces)
    part[0, :, :slab] = product[:RANK]
    part[1, :, :slab] = -product[RANK:]
    part[0, :, slab : slab + RANK] = 0.5 * gram[:RANK, :RANK]
    part[1, :, slab : slab + RANK] = 0.5 * gram[RANK:, RANK:]

    z_copies = [
        send(part.at[0], zbuf.at[core], zsend.at[0], zrecv.at[core], (right, chip + 1)),
        send(part.at[1], zbuf.at[core], zsend.at[1], zrecv.at[core], (left, chip)),
        send(part.at[1 - core], zbuf.at[2], zsend.at[2], zrecv.at[2], (r, chip + 1 - core)),
    ]
    for i, (lo, size) in enumerate(chunks):
        high, mid, low = saved[i]
        stack = jnp.concatenate([high, high, high, mid, mid, low], axis=0)
        columns = stack.T
        for p in range(lo // tall_rows, (lo + size) // tall_rows):
            images[p][...] = columns[p * tall_rows - lo : (p + 1) * tall_rows - lo]

    def landed(buf, sem):
        pltpu.make_async_remote_copy(
            src_ref=buf, dst_ref=buf, send_sem=zsend.at[0], recv_sem=sem,
            device_id=(r, chip + 1 - core), device_id_type=MESH,
        ).wait_recv()

    for k in range(3):
        landed(zbuf.at[k], zrecv.at[k])
    zsum[...] = (part[core] + zbuf[2]) + (zbuf[0] + zbuf[1])

    x_copies = []
    for k in range(1, X):
        peer = lax.rem(x + k, X)
        x_copies.append(send(zsum, xbuf.at[x], xsend.at[k - 1], xrecv.at[x], (r, at(y, peer, core))))
    xbuf[x] = zsum[...]
    for k in range(1, X):
        slot = lax.rem(x + k, X)
        landed(xbuf.at[slot], xrecv.at[slot])
    xsum[...] = (xbuf[0] + xbuf[1]) + (xbuf[2] + xbuf[3])

    y_copies = []
    for k in range(1, Y):
        peer = lax.rem(y + k, Y)
        for cc in range(C):
            y_copies.append(
                send(
                    xsum, ybuf.at[core, y], ysend.at[1 + (k - 1) * C + cc], yrecv.at[core, y],
                    (r, at(peer, x, cc)),
                )
            )
    y_copies.append(
        send(xsum, ybuf.at[core, y], ysend.at[0], yrecv.at[core, y], (r, chip + 1 - core))
    )
    ybuf[core, y] = xsum[...]
    landed(ybuf.at[1 - core, y], yrecv.at[1 - core, y])
    for k in range(1, Y):
        slot = lax.rem(y + k, Y)
        for cc in range(C):
            landed(ybuf.at[cc, slot], yrecv.at[cc, slot])

    rows = lax.broadcasted_iota(jnp.int32, (RANK, 1), 0)
    work = [(ybuf[e, 0] + ybuf[e, 1]) + (ybuf[e, 2] + ybuf[e, 3]) for e in range(2)]
    ends = [[], []]
    for j in range(RANK):
        for e in range(2):
            a = work[e]
            column = a[:, slab + j : slab + j + 1]
            pivot = column[j : j + 1, :]
            row = a[j : j + 1, :]
            if e == 0:
                next_ref[j : j + 1, :] = row[:, :slab] / jnp.sqrt(pivot)
            work[e] = a - jnp.where(rows == j, 0.0, column / pivot) * row
            ends[e].append(pivot)
    kept = [work[e][:, :slab] / jnp.concatenate(ends[e], axis=0) for e in range(2)]
    mix_ref[:RANK] = mix_rate * kept[0]
    mix_ref[RANK:] = -mix_rate * kept[1]
    for pair in image_copies:
        for copy in pair:
            copy.wait_send()
    for copy in z_copies + x_copies + y_copies:
        copy.wait_send()


def finish(*refs):
    steps, images = refs[:PIECES], refs[PIECES : 2 * PIECES]
    mix_v, next_v, out_hbm, next_hbm, out_v, sems = refs[2 * PIECES :]
    tall = steps[0].shape[0]
    last = pltpu.make_async_copy(next_v, next_hbm, sems.at[PIECES])
    last.start()
    high, mid, low = split3(mix_v[...])
    mix_stack = jnp.concatenate([high, mid, low, high, mid, high], axis=0)
    stores = [last]
    for p in range(PIECES):
        span = pl.ds(p * tall, tall)
        out_v[span, :] = steps[p][...] - dot(images[p][...], mix_stack, ((1,), (0,)))
        store = pltpu.make_async_copy(out_v.at[span], out_hbm.at[span], sems.at[p])
        store.start()
        stores.append(store)
    for store in stores:
        store.wait()


def local(count, weights, hidden, grad_out, warm_start):
    _, rows, slab = weights.shape
    tokens = hidden.shape[0]
    factor = step_rate / math.sqrt(tokens)
    chunks = [(0, 512), (512, rows - 512)]
    n = len(chunks)
    wide = slab + 128
    terms = 12 * RANK
    in_vmem = pl.BlockSpec(memory_space=pltpu.VMEM)
    in_hbm = pl.BlockSpec(memory_space=pltpu.HBM)
    kept = pl.pallas_call(
        functools.partial(kernel, count, chunks, factor),
        out_shape=(
            *[jax.ShapeDtypeStruct((rows // PIECES, slab), F32)] * PIECES,
            *[jax.ShapeDtypeStruct((rows // PIECES, terms), BF16)] * PIECES,
            jax.ShapeDtypeStruct((2 * RANK, slab), F32),
            jax.ShapeDtypeStruct((RANK, slab), F32),
        ),
        in_specs=[in_hbm] * 4,
        out_specs=(in_vmem,) * (2 * PIECES + 2),
        scratch_shapes=[
            pltpu.VMEM((rows, slab), F32),
            pltpu.VMEM((tokens, rows), BF16),
            pltpu.VMEM((tokens, slab), BF16),
            pltpu.VMEM((2, RANK, slab), F32),
            pltpu.VMEM((3, rows, slab), BF16),
            pltpu.VMEM((2, RANK, rows), F32),
            pltpu.VMEM((2, RANK, rows), F32),
            pltpu.VMEM((2, RANK, wide), F32),
            pltpu.VMEM((3, RANK, wide), F32),
            pltpu.VMEM((RANK, wide), F32),
            pltpu.VMEM((X, RANK, wide), F32),
            pltpu.VMEM((RANK, wide), F32),
            pltpu.VMEM((C, Y, RANK, wide), F32),
            pltpu.SemaphoreType.DMA((3 + 2 * n,)),
            pltpu.SemaphoreType.DMA((2 * n,)),
            pltpu.SemaphoreType.DMA((2 * n,)),
            pltpu.SemaphoreType.DMA((3,)),
            pltpu.SemaphoreType.DMA((3,)),
            pltpu.SemaphoreType.DMA((X - 1,)),
            pltpu.SemaphoreType.DMA((X,)),
            pltpu.SemaphoreType.DMA((1 + (Y - 1) * C,)),
            pltpu.SemaphoreType.DMA((C, Y)),
        ],
        compiler_params=pltpu.CompilerParams(
            collective_id=0, has_side_effects=True, vmem_limit_bytes=53480 * 1024
        ),
    )(weights[0], hidden, grad_out, warm_start)
    new_weights, next_start = pl.pallas_call(
        finish,
        out_shape=(
            jax.ShapeDtypeStruct((rows, slab), F32),
            jax.ShapeDtypeStruct((RANK, slab), F32),
        ),
        in_specs=[in_vmem] * (2 * PIECES + 2),
        out_specs=(in_hbm,) * 2,
        scratch_shapes=[
            pltpu.VMEM((rows, slab), F32),
            pltpu.SemaphoreType.DMA((PIECES + 1,)),
        ],
        compiler_params=pltpu.CompilerParams(vmem_limit_bytes=53480 * 1024),
    )(*kept)
    return new_weights[None], next_start[None]


def solution(mesh):
    return jax.shard_map(
        functools.partial(local, mesh.shape["blk"]),
        mesh=mesh,
        in_specs=(P("blk", "tp", None), P("blk", "tp"), P("blk", None), P()),
        out_specs=(P("blk", "tp", None), P("blk", None, None)),
        check_vma=False,
    )
```

time: 234 us -> 31.6 us (0.14); the launches traced: 230 us -> 31.4 us
  blocking collectives: 187 us -> 0 us
  Pallas kernels: 0 us -> 30.7 us
  waiting for transfers between devices: 14.8 us -> 0 us
  starting transfers between devices: 14.2 us -> 0 us
  matrix products: 8.83 us -> 0 us
  other arithmetic: 2.57 us -> 0 us
    psum x2 -> x0, blocking collectives: 187 us -> none  [the longest x1 121 us: local(): back_products = lax.psum(partial_back, 'tp')]
    pallas_call x0 -> x2, Pallas kernels: none -> 30.7 us  [the longest x1 29.4 us: local(): pl.pallas_call(functools.partial(kernel, count, chunks, factor), out_shap...]
    ppermute x4 -> x0, waiting for transfers between devices: 14.8 us -> none  [the longest x2 12.7 us: padded_2(): lax.ppermute(tail, axis, [(i, (i + 1) % count) for i in range(count)])]
    ppermute x4 -> x0, starting transfers between devices: 14.2 us -> none  [the longest x2 7.92 us: padded_2(): lax.ppermute(head, axis, [((i + 1) % count, i) for i in range(count)])]
    dot_general x6 -> x0, matrix products: 8.83 us -> none  [the longest x1 2.72 us: local(): lax.dot_general(hidden, grad_out, (((0,), (0,)), ((), ())), preferred_ele...]
  transfers between devices with their start and end apart: 4 -> 0, of which waited for: 4 -> 0; matrix products, arithmetic and copies ran while one was open for 0% -> 0% of each run, Pallas kernels for 0% -> 0%
where the time goes in v1:
time: 31.6 us; the launch traced here: 31.4 us
  Pallas kernels  30.7 us (97%)
  between operations  0.64 us (2%)
    pallas_call x1, Pallas kernels, local(): pl.pallas_call(functools.partial(kernel, count, chunks, factor), out_shap...  29.4 us
    pallas_call x1, Pallas kernels, local(): pl.pallas_call(finish, out_shape=(jax.ShapeDtypeStruct((rows, slab), F32)...  1.38 us

profile of v1, /device:TPU:1, one launch (start us, length us, event | category | flops | bytes accessed | tf_op | source)
XLA Modules:
  0.0 31.4 jit_solution(12035974308415835888)
XLA Ops:
  0.6 29.4 %shard_map.59 = (f32[64,384]{1,0:T(8,128)S(1)}, f32[64,384]{1,0:T(8,128)S(1)}, f32[64,384]{1,0:T(8,128)S(1)}, f32[64,384]{1,0:T(8,128)S(1)}, f32[64,384]{1,0:T(8...) custom-call(f32[896,384]{1,0:T(8,128)} %bitcast.3, ...), custom_call_target="tpu_custom_call" | custom-call | tf_op jit(solution)/shard_map/pallas_call | solution.py:263
  30.0 1.4 %shard_map.60 = (f32[896,384]{1,0:T(8,128)}, f32[8,384]{1,0:T(8,128)}) custom-call(f32[64,384]{1,0:T(8,128)S(1)} %get-tuple-element.34.refs_0_, f32[64,384]{1,0:T(8,128)S(1)} %get-tuple-element.35.refs_1_, f32[64,384]{1,0:T(8,128)S(1)} %get-tuple-element.36.refs_2_, f32[64,384]{1,0:T(8,128)S(1)} %get-tuple-element.37.refs_3_, ...), custom_call_target="tpu_custom_call" | custom-call | tf_op jit(solution)/shard_map/pallas_call | solution.py:301

commit v2 on v1

v2 whole, which is shorter than its diff:
```python
import functools
import math

import jax
import jax.numpy as jnp
from jax import lax
from jax.experimental import pallas as pl
from jax.experimental.pallas import tpu as pltpu
from jax.sharding import PartitionSpec as P

step_rate = 0.5
mix_rate = 0.5
MESH = pl.DeviceIdType.MESH
X, Y, C = 4, 4, 2
RANK = 8
PIECES = 14
F32, BF16 = jnp.float32, jnp.bfloat16


def split3(v):
    high = v.astype(BF16)
    rest = v - high.astype(F32)
    mid = rest.astype(BF16)
    low = (rest - mid.astype(F32)).astype(BF16)
    return high, mid, low


def dot(a, b, dims):
    return lax.dot_general(a, b, (dims, ((), ())), preferred_element_type=F32)


def folded(v):
    n = v.shape[0] // 3
    return v[:n] + (v[n : 2 * n] + v[2 * n :])


def send(src, dst, send_sem, recv_sem, peer):
    copy = pltpu.make_async_remote_copy(
        src_ref=src, dst_ref=dst, send_sem=send_sem, recv_sem=recv_sem,
        device_id=peer, device_id_type=MESH,
    )
    copy.start()
    return copy


def kernel(
    count, chunks, factor,
    w_hbm, h_hbm, g_hbm, s_hbm, *rest,
):
    steps, images, rest = rest[:PIECES], rest[PIECES : 2 * PIECES], rest[2 * PIECES :]
    mix_ref, next_ref, w_v, h_v, g_v, start_v, parts_v, own, land, part = rest[:10]
    first, second, load_sems, isend, irecv, sends, recvs = rest[10:]
    tall_rows = steps[0].shape[0]
    r = lax.axis_index("blk")
    t = lax.axis_index("tp")
    core = lax.rem(t, C)
    x = lax.rem(lax.div(t, C), X)
    y = lax.div(t, C * X)
    right = lax.rem(r + 1, count)
    left = lax.rem(r + count - 1, count)
    chip = t - core
    slab = w_v.shape[1]

    def at(yy, xx, cc):
        return (yy * X + xx) * C + cc

    loads = [
        pltpu.make_async_copy(s_hbm.at[r], start_v.at[0], load_sems.at[1]),
        pltpu.make_async_copy(s_hbm.at[left], start_v.at[1], load_sems.at[2]),
        pltpu.make_async_copy(g_hbm, g_v, load_sems.at[0]),
    ]
    for copy in loads:
        copy.start()
    chunk_loads = []
    for i, (lo, size) in enumerate(chunks):
        w_copy = pltpu.make_async_copy(
            w_hbm.at[pl.ds(lo, size)], w_v.at[pl.ds(lo, size)], load_sems.at[4 + 2 * i]
        )
        h_copy = pltpu.make_async_copy(
            h_hbm.at[:, pl.ds(lo, size)], h_v.at[:, pl.ds(lo, size)], load_sems.at[3 + 2 * i]
        )
        w_copy.start()
        h_copy.start()
        chunk_loads.append((w_copy, h_copy))

    barrier = pltpu.get_barrier_semaphore()
    def turned(v, k, size):
        return lax.rem(v + k, size)

    peers = []
    for kx in range(X):
        for cc in range(C):
            for side in (left, right):
                peers.append((side, at(y, turned(x, kx, X), cc)))
    around = [(ky, kx, kc) for ky in range(Y) for kx in range(X) for kc in range(C)][1:]
    for ky, kx, kc in around:
        peers.append((r, at(turned(y, ky, Y), turned(x, kx, X), turned(core, kc, C))))
    for peer in peers:
        pl.semaphore_signal(barrier, inc=1, device_id=peer, device_id_type=MESH)

    part[...] = jnp.zeros_like(part)
    for copy in loads:
        copy.wait()
    starts = start_v[...].reshape(2 * RANK, slab)
    start_parts = split3(starts)
    tall = jnp.concatenate(start_parts, axis=0)
    n = 2 * RANK
    tall_t = tall.T
    grad_t = g_v[...].T
    felt = factor * folded(dot(tall, grad_t, ((1,), (0,))))
    felt_tall = jnp.concatenate(split3(felt), axis=0)

    image_copies = []
    for i, (lo, size) in enumerate(chunks):
        span = pl.ds(lo, size)
        chunk_loads[i][0].wait()
        high, mid, low = [dot(v, tall_t, ((1,), (0,))) for v in split3(w_v[span, :])]
        seen = (high + (mid + low)).T
        chunk_loads[i][1].wait()
        image = folded(seen - dot(felt_tall, h_v[:, span], ((1,), (0,))))
        own[0, :, span] = image[:RANK]
        own[1, :, span] = image[RANK:]
        if i == 0:
            pl.semaphore_wait(barrier, len(peers))
        image_copies.append(
            (
                send(own.at[0, :, span], land.at[1, :, span], isend.at[2 * i], irecv.at[2 * i], (right, t)),
                send(own.at[1, :, span], land.at[0, :, span], isend.at[2 * i + 1], irecv.at[2 * i + 1], (left, t)),
            )
        )

    for lo, size in chunks:
        span = pl.ds(lo, size)
        gradient = dot(grad_t, h_v[:, span], ((1,), (0,)))
        stepped = w_v[span, :] - factor * gradient.T
        for p in range(lo // tall_rows, (lo + size) // tall_rows):
            steps[p][...] = stepped[p * tall_rows - lo : (p + 1) * tall_rows - lo]
        stacks = split3(stepped)
        for k in range(3):
            parts_v[k, span, :] = stacks[k]

    product = jnp.zeros((3 * n, slab), F32)
    gram = jnp.zeros((3 * n, n), F32)
    saved = []
    for i, (lo, size) in enumerate(chunks):
        span = pl.ds(lo, size)
        for copy in image_copies[i]:
            copy.wait_recv()
        edge = [own[0, :, span] - land[0, :, span], land[1, :, span] - own[1, :, span]]
        pieces = split3(jnp.concatenate(edge, axis=0))
        rows = jnp.concatenate(pieces, axis=0)
        for k in range(3):
            product = product + dot(rows, parts_v[k, span, :], ((1,), (0,)))
            gram = gram + dot(rows, pieces[k], ((1,), (1,)))
        saved.append(pieces)
    product, gram = folded(product), folded(gram)
    for k in range(X - 1):
        part[0, k] = product[:RANK, 128 * k : 128 * (k + 1)]
        part[1, k] = -product[RANK:, 128 * k : 128 * (k + 1)]
    part[0, X - 1, :, :RANK] = 0.5 * gram[:RANK, :RANK]
    part[1, X - 1, :, :RANK] = 0.5 * gram[RANK:, RANK:]

    for kx in reversed(range(X)):
        tile = turned(x, kx, X)
        back = (-kx) % X
        slot = X * C + C * back + core
        send(part.at[0, tile], first.at[slot], sends.at[0], recvs.at[0], (right, at(y, tile, 1)))
        send(part.at[1, tile], first.at[slot], sends.at[0], recvs.at[0], (left, at(y, tile, 0)))
        for kc in range(C):
            if kx or kc:
                edge = turned(core, kc, C)
                send(part.at[edge, tile], first.at[C * back + kc], sends.at[0], recvs.at[0], (r, at(y, tile, edge)))
    first[0] = part[core, x]
    for i, (lo, size) in enumerate(chunks):
        high, mid, low = saved[i]
        stack = jnp.concatenate([high, high, high, mid, mid, low], axis=0)
        columns = stack.T
        for p in range(lo // tall_rows, (lo + size) // tall_rows):
            images[p][...] = columns[p * tall_rows - lo : (p + 1) * tall_rows - lo]

    def whole(buf, step):
        return pltpu.make_async_remote_copy(
            src_ref=buf, dst_ref=buf, send_sem=sends.at[step], recv_sem=recvs.at[step],
            device_id=(r, chip + 1 - core), device_id_type=MESH,
        )

    early = first.at[pl.ds(1, first.shape[0] - 1)]
    late = second.at[pl.ds(1, second.shape[0] - 1)]
    whole(early, 0).wait_recv()
    terms = [first[k] for k in range(first.shape[0])]
    while len(terms) > 1:
        terms = [a + b for a, b in zip(terms[::2], terms[1::2])]
    second[0] = terms[0]
    for ky, kx, kc in reversed(around):
        send(
            second.at[0], second.at[(((-ky) % Y) * X + (-kx) % X) * C + kc], sends.at[1], recvs.at[1],
            (r, at(turned(y, ky, Y), turned(x, kx, X), turned(core, kc, C))),
        )
    whole(late, 1).wait_recv()

    def total(e, tile):
        kx = lax.rem(tile - x + X, X)
        kc = lax.rem(e + core, C)
        own = [second[(lax.rem(k - y + Y, Y) * X + kx) * C + kc] for k in range(Y)]
        return (own[0] + own[1]) + (own[2] + own[3])

    place = lax.broadcasted_iota(jnp.int32, (RANK, 128), 0)
    gram = [total(e, X - 1) for e in range(2)]
    right_side = [[total(e, k) for k in range(X - 1)] for e in range(2)]
    columns = [[jnp.broadcast_to(a[:, j : j + 1], (RANK, 128)) for j in range(RANK)] for a in gram]

    def spread(v, j):
        return jnp.broadcast_to(v[j : j + 1, :], (RANK, 128))

    ends = [jnp.ones((RANK, 128), F32)] * 2
    for j in range(RANK):
        for e in range(2):
            pivot = spread(columns[e][j], j)
            scale = jnp.where(place == j, 0.0, columns[e][j] * (1.0 / pivot))
            if e == 0:
                root = 1.0 / jnp.sqrt(pivot[:1])
                for k, v in enumerate(right_side[e]):
                    next_ref[j : j + 1, 128 * k : 128 * (k + 1)] = v[j : j + 1, :] * root
            for k in range(j + 1, RANK):
                columns[e][k] = columns[e][k] - scale * spread(columns[e][k], j)
            right_side[e] = [v - scale * spread(v, j) for v in right_side[e]]
            ends[e] = jnp.where(place == j, pivot, ends[e])
    for e, sign in enumerate((mix_rate, -mix_rate)):
        inverse = sign / ends[e]
        for k, v in enumerate(right_side[e]):
            mix_ref[RANK * e : RANK * (e + 1), 128 * k : 128 * (k + 1)] = v * inverse
    for pair in image_copies:
        for copy in pair:
            copy.wait_send()
    whole(early, 0).wait_send()
    whole(late, 1).wait_send()


def finish(*refs):
    steps, images = refs[:PIECES], refs[PIECES : 2 * PIECES]
    mix_v, next_v, out_hbm, next_hbm, out_v, sems = refs[2 * PIECES :]
    tall = steps[0].shape[0]
    last = pltpu.make_async_copy(next_v, next_hbm, sems.at[PIECES])
    last.start()
    high, mid, low = split3(mix_v[...])
    mix_stack = jnp.concatenate([high, mid, low, high, mid, high], axis=0)
    stores = [last]
    for p in range(PIECES):
        span = pl.ds(p * tall, tall)
        out_v[span, :] = steps[p][...] - dot(images[p][...], mix_stack, ((1,), (0,)))
        store = pltpu.make_async_copy(out_v.at[span], out_hbm.at[span], sems.at[p])
        store.start()
        stores.append(store)
    for store in stores:
        store.wait()


def local(count, weights, hidden, grad_out, warm_start):
    _, rows, slab = weights.shape
    tokens = hidden.shape[0]
    factor = step_rate / math.sqrt(tokens)
    chunks = [(0, 512), (512, rows - 512)]
    n = len(chunks)
    terms = 12 * RANK
    in_vmem = pl.BlockSpec(memory_space=pltpu.VMEM)
    in_hbm = pl.BlockSpec(memory_space=pltpu.HBM)
    kept = pl.pallas_call(
        functools.partial(kernel, count, chunks, factor),
        out_shape=(
            *[jax.ShapeDtypeStruct((rows // PIECES, slab), F32)] * PIECES,
            *[jax.ShapeDtypeStruct((rows // PIECES, terms), BF16)] * PIECES,
            jax.ShapeDtypeStruct((2 * RANK, slab), F32),
            jax.ShapeDtypeStruct((RANK, slab), F32),
        ),
        in_specs=[in_hbm] * 4,
        out_specs=(in_vmem,) * (2 * PIECES + 2),
        scratch_shapes=[
            pltpu.VMEM((rows, slab), F32),
            pltpu.VMEM((tokens, rows), BF16),
            pltpu.VMEM((tokens, slab), BF16),
            pltpu.VMEM((2, RANK, slab), F32),
            pltpu.VMEM((3, rows, slab), BF16),
            pltpu.VMEM((2, RANK, rows), F32),
            pltpu.VMEM((2, RANK, rows), F32),
            pltpu.VMEM((2, X, RANK, 128), F32),
            pltpu.VMEM((2 * X * C, RANK, 128), F32),
            pltpu.VMEM((Y * X * C, RANK, 128), F32),
            pltpu.SemaphoreType.DMA((3 + 2 * n,)),
            pltpu.SemaphoreType.DMA((2 * n,)),
            pltpu.SemaphoreType.DMA((2 * n,)),
            pltpu.SemaphoreType.DMA((2,)),
            pltpu.SemaphoreType.DMA((2,)),
        ],
        compiler_params=pltpu.CompilerParams(
            collective_id=0, has_side_effects=True, vmem_limit_bytes=53480 * 1024
        ),
    )(weights[0], hidden, grad_out, warm_start)
    new_weights, next_start = pl.pallas_call(
        finish,
        out_shape=(
            jax.ShapeDtypeStruct((rows, slab), F32),
            jax.ShapeDtypeStruct((RANK, slab), F32),
        ),
        in_specs=[in_vmem] * (2 * PIECES + 2),
        out_specs=(in_hbm,) * 2,
        scratch_shapes=[
            pltpu.VMEM((rows, slab), F32),
            pltpu.SemaphoreType.DMA((PIECES + 1,)),
        ],
        compiler_params=pltpu.CompilerParams(vmem_limit_bytes=53480 * 1024),
    )(*kept)
    return new_weights[None], next_start[None]


def solution(mesh):
    return jax.shard_map(
        functools.partial(local, mesh.shape["blk"]),
        mesh=mesh,
        in_specs=(P("blk", "tp", None), P("blk", "tp"), P("blk", None), P()),
        out_specs=(P("blk", "tp", None), P("blk", None, None)),
        check_vma=False,
    )
```

time: 31.6 us -> 31.1 us (0.984)
  Pallas kernels: 30.7 us -> 30.2 us
    pallas_call x1, Pallas kernels: 29.4 us -> 28.9 us  [local(): pl.pallas_call(functools.partial(kernel, count, chunks, factor), out_shap...]
where the time goes in v2:
time: 31.1 us; the launch traced here: 30.9 us
  Pallas kernels  30.2 us (97%)
  between operations  0.64 us (2%)
    pallas_call x1, Pallas kernels, local(): pl.pallas_call(functools.partial(kernel, count, chunks, factor), out_shap...  28.9 us
    pallas_call x1, Pallas kernels, local(): pl.pallas_call(finish, out_shape=(jax.ShapeDtypeStruct((rows, slab), F32)...  1.38 us

profile of v2, /device:TPU:1, one launch (start us, length us, event | category | flops | bytes accessed | tf_op | source)
XLA Modules:
  0.0 30.9 jit_solution(653581172011283771)
XLA Ops:
  0.6 28.9 %shard_map.59 = (f32[64,384]{1,0:T(8,128)S(1)}, f32[64,384]{1,0:T(8,128)S(1)}, f32[64,384]{1,0:T(8,128)S(1)}, f32[64,384]{1,0:T(8,128)S(1)}, f32[64,384]{1,0:T(8...) custom-call(f32[896,384]{1,0:T(8,128)} %bitcast.3, ...), custom_call_target="tpu_custom_call" | custom-call | tf_op jit(solution)/shard_map/pallas_call | solution.py:267
  29.5 1.4 %shard_map.60 = (f32[896,384]{1,0:T(8,128)}, f32[8,384]{1,0:T(8,128)}) custom-call(f32[64,384]{1,0:T(8,128)S(1)} %get-tuple-element.34.refs_0_, f32[64,384]{1,0:T(8,128)S(1)} %get-tuple-element.35.refs_1_, f32[64,384]{1,0:T(8,128)S(1)} %get-tuple-element.36.refs_2_, f32[64,384]{1,0:T(8,128)S(1)} %get-tuple-element.37.refs_3_, ...), custom_call_target="tpu_custom_call" | custom-call | tf_op jit(solution)/shard_map/pallas_call | solution.py:298

commit v3 on v2

--- a/solution.py
+++ b/solution.py
@@ -80,8 +80,9 @@
             h_hbm.at[:, pl.ds(lo, size)], h_v.at[:, pl.ds(lo, size)], load_sems.at[3 + 2 * i]
         )
         w_copy.start()
-        h_copy.start()
         chunk_loads.append((w_copy, h_copy))
+    for pair in chunk_loads:
+        pair[1].start()
 
     barrier = pltpu.get_barrier_semaphore()
     def turned(v, k, size):
@@ -110,14 +111,16 @@
     felt = factor * folded(dot(tall, grad_t, ((1,), (0,))))
     felt_tall = jnp.concatenate(split3(felt), axis=0)
 
+    seen = []
+    for i, (lo, size) in enumerate(chunks):
+        chunk_loads[i][0].wait()
+        high, mid, low = [dot(v, tall_t, ((1,), (0,))) for v in split3(w_v[pl.ds(lo, size), :])]
+        seen.append(folded((high + (mid + low)).T))
     image_copies = []
     for i, (lo, size) in enumerate(chunks):
         span = pl.ds(lo, size)
-        chunk_loads[i][0].wait()
-        high, mid, low = [dot(v, tall_t, ((1,), (0,))) for v in split3(w_v[span, :])]
-        seen = (high + (mid + low)).T
         chunk_loads[i][1].wait()
-        image = folded(seen - dot(felt_tall, h_v[:, span], ((1,), (0,))))
+        image = seen[i] - folded(dot(felt_tall, h_v[:, span], ((1,), (0,))))
         own[0, :, span] = image[:RANK]
         own[1, :, span] = image[RANK:]
         if i == 0:
@@ -139,45 +142,46 @@
         for k in range(3):
             parts_v[k, span, :] = stacks[k]
 
-    product = jnp.zeros((3 * n, slab), F32)
-    gram = jnp.zeros((3 * n, n), F32)
-    saved = []
-    for i, (lo, size) in enumerate(chunks):
-        span = pl.ds(lo, size)
-        for copy in image_copies[i]:
-            copy.wait_recv()
-        edge = [own[0, :, span] - land[0, :, span], land[1, :, span] - own[1, :, span]]
-        pieces = split3(jnp.concatenate(edge, axis=0))
-        rows = jnp.concatenate(pieces, axis=0)
-        for k in range(3):
-            product = product + dot(rows, parts_v[k, span, :], ((1,), (0,)))
-            gram = gram + dot(rows, pieces[k], ((1,), (1,)))
-        saved.append(pieces)
-    product, gram = folded(product), folded(gram)
-    for k in range(X - 1):
-        part[0, k] = product[:RANK, 128 * k : 128 * (k + 1)]
-        part[1, k] = -product[RANK:, 128 * k : 128 * (k + 1)]
-    part[0, X - 1, :, :RANK] = 0.5 * gram[:RANK, :RANK]
-    part[1, X - 1, :, :RANK] = 0.5 * gram[RANK:, RANK:]
-
-    for kx in reversed(range(X)):
-        tile = turned(x, kx, X)
-        back = (-kx) % X
-        slot = X * C + C * back + core
-        send(part.at[0, tile], first.at[slot], sends.at[0], recvs.at[0], (right, at(y, tile, 1)))
-        send(part.at[1, tile], first.at[slot], sends.at[0], recvs.at[0], (left, at(y, tile, 0)))
-        for kc in range(C):
-            if kx or kc:
-                edge = turned(core, kc, C)
-                send(part.at[edge, tile], first.at[C * back + kc], sends.at[0], recvs.at[0], (r, at(y, tile, edge)))
+    images_f = [[], []]
+    for e in range(2):
+        product = jnp.zeros((3 * RANK, slab), F32)
+        gram = jnp.zeros((3 * RANK, RANK), F32)
+        for i, (lo, size) in enumerate(chunks):
+            span = pl.ds(lo, size)
+            image_copies[i][1 - e].wait_recv()
+            image = own[0, :, span] - land[0, :, span] if e == 0 else land[1, :, span] - own[1, :, span]
+            images_f[e].append(image)
+            pieces = split3(image)
+            rows = jnp.concatenate([v.astype(F32) for v in pieces], axis=0).astype(BF16)
+            for k in range(3):
+                product = product + dot(rows, parts_v[k, span, :], ((1,), (0,)))
+                gram = gram + dot(rows, pieces[k], ((1,), (1,)))
+        product, gram = folded(product), folded(gram)
+        for k in range(X - 1):
+            block = product[:, 128 * k : 128 * (k + 1)]
+            part[e, k] = block if e == 0 else -block
+        part[e, X - 1, :, :RANK] = 0.5 * gram
+        aside = lax.rem(core + e, C)
+        for kx in reversed(range(X)):
+            tile = turned(x, kx, X)
+            back = (-kx) % X
+            side, taker = ((right, 1), (left, 0))[e]
+            send(
+                part.at[e, tile], first.at[X * C + C * back + core], sends.at[0], recvs.at[0],
+                (side, at(y, tile, taker)),
+            )
+
+            def near():
+                send(
+                    part.at[e, tile], first.at[C * back + aside], sends.at[0], recvs.at[0],
+                    (r, at(y, tile, e)),
+                )
+
+            if kx:
+                near()
+            else:
+                pl.when(core != e)(near)
     first[0] = part[core, x]
-    for i, (lo, size) in enumerate(chunks):
-        high, mid, low = saved[i]
-        stack = jnp.concatenate([high, high, high, mid, mid, low], axis=0)
-        columns = stack.T
-        for p in range(lo // tall_rows, (lo + size) // tall_rows):
-            images[p][...] = columns[p * tall_rows - lo : (p + 1) * tall_rows - lo]
-
     def whole(buf, step):
         return pltpu.make_async_remote_copy(
             src_ref=buf, dst_ref=buf, send_sem=sends.at[step], recv_sem=recvs.at[step],
@@ -196,6 +200,12 @@
             second.at[0], second.at[(((-ky) % Y) * X + (-kx) % X) * C + kc], sends.at[1], recvs.at[1],
             (r, at(turned(y, ky, Y), turned(x, kx, X), turned(core, kc, C))),
         )
+    for i, (lo, size) in enumerate(chunks):
+        high, mid, low = split3(jnp.concatenate([images_f[0][i], images_f[1][i]], axis=0))
+        stack = jnp.concatenate([high, high, high, mid, mid, low], axis=0)
+        columns = stack.T
+        for p in range(lo // tall_rows, (lo + size) // tall_rows):
+            images[p][...] = columns[p * tall_rows - lo : (p + 1) * tall_rows - lo]
     whole(late, 1).wait_recv()
 
     def total(e, tile):

time: 31.1 us -> 30.5 us (0.981)
  Pallas kernels: 30.2 us -> 29.7 us
    pallas_call x1, Pallas kernels: 28.9 us -> 28.3 us  [local(): pl.pallas_call(functools.partial(kernel, count, chunks, factor), out_shap...]
where the time goes in v3:
time: 30.5 us; the launch traced here: 30.3 us
  Pallas kernels  29.7 us (97%)
  between operations  0.64 us (2%)
    pallas_call x1, Pallas kernels, local(): pl.pallas_call(functools.partial(kernel, count, chunks, factor), out_shap...  28.3 us
    pallas_call x1, Pallas kernels, local(): pl.pallas_call(finish, out_shape=(jax.ShapeDtypeStruct((rows, slab), F32)...  1.38 us

profile of v3, /device:TPU:1, one launch (start us, length us, event | category | flops | bytes accessed | tf_op | source)
XLA Modules:
  0.0 30.3 jit_solution(14180596319029173389)
XLA Ops:
  0.6 28.3 %shard_map.59 = (f32[64,384]{1,0:T(8,128)S(1)}, f32[64,384]{1,0:T(8,128)S(1)}, f32[64,384]{1,0:T(8,128)S(1)}, f32[64,384]{1,0:T(8,128)S(1)}, f32[64,384]{1,0:T(8...) custom-call(f32[896,384]{1,0:T(8,128)} %bitcast.3, ...), custom_call_target="tpu_custom_call" | custom-call | tf_op jit(solution)/shard_map/pallas_call | solution.py:277
  28.9 1.4 %shard_map.60 = (f32[896,384]{1,0:T(8,128)}, f32[8,384]{1,0:T(8,128)}) custom-call(f32[64,384]{1,0:T(8,128)S(1)} %get-tuple-element.34.refs_0_, f32[64,384]{1,0:T(8,128)S(1)} %get-tuple-element.35.refs_1_, f32[64,384]{1,0:T(8,128)S(1)} %get-tuple-element.36.refs_2_, f32[64,384]{1,0:T(8,128)S(1)} %get-tuple-element.37.refs_3_, ...), custom_call_target="tpu_custom_call" | custom-call | tf_op jit(solution)/shard_map/pallas_call | solution.py:308

commit v4 on v3

--- a/solution.py
+++ b/solution.py
@@ -94,10 +94,16 @@
             for side in (left, right):
                 peers.append((side, at(y, turned(x, kx, X), cc)))
     around = [(ky, kx, kc) for ky in range(Y) for kx in range(X) for kc in range(C)][1:]
+    around.sort(key=lambda k: -min(k[0], Y - k[0]) - min(k[1], X - k[1]))
+    along_x = sorted(range(X), key=lambda k: -min(k, X - k))
     for ky, kx, kc in around:
         peers.append((r, at(turned(y, ky, Y), turned(x, kx, X), turned(core, kc, C))))
-    for peer in peers:
-        pl.semaphore_signal(barrier, inc=1, device_id=peer, device_id_type=MESH)
+
+    def greet(some):
+        for peer in some:
+            pl.semaphore_signal(barrier, inc=1, device_id=peer, device_id_type=MESH)
+
+    greet(peers[: 2 * X * C])
 
     part[...] = jnp.zeros_like(part)
     for copy in loads:
@@ -110,6 +116,7 @@
     grad_t = g_v[...].T
     felt = factor * folded(dot(tall, grad_t, ((1,), (0,))))
     felt_tall = jnp.concatenate(split3(felt), axis=0)
+    greet(peers[2 * X * C :])
 
     seen = []
     for i, (lo, size) in enumerate(chunks):
@@ -162,18 +169,19 @@
             part[e, k] = block if e == 0 else -block
         part[e, X - 1, :, :RANK] = 0.5 * gram
         aside = lax.rem(core + e, C)
-        for kx in reversed(range(X)):
+        side, taker = ((right, 1), (left, 0))[e]
+        for kx in along_x:
             tile = turned(x, kx, X)
-            back = (-kx) % X
-            side, taker = ((right, 1), (left, 0))[e]
             send(
-                part.at[e, tile], first.at[X * C + C * back + core], sends.at[0], recvs.at[0],
+                part.at[e, tile], first.at[X * C + C * ((-kx) % X) + core], sends.at[0], recvs.at[0],
                 (side, at(y, tile, taker)),
             )
+        for kx in along_x:
+            tile = turned(x, kx, X)
 
             def near():
                 send(
-                    part.at[e, tile], first.at[C * back + aside], sends.at[0], recvs.at[0],
+                    part.at[e, tile], first.at[C * ((-kx) % X) + aside], sends.at[0], recvs.at[0],
                     (r, at(y, tile, e)),
                 )
 
@@ -195,7 +203,7 @@
     while len(terms) > 1:
         terms = [a + b for a, b in zip(terms[::2], terms[1::2])]
     second[0] = terms[0]
-    for ky, kx, kc in reversed(around):
+    for ky, kx, kc in around:
         send(
             second.at[0], second.at[(((-ky) % Y) * X + (-kx) % X) * C + kc], sends.at[1], recvs.at[1],
             (r, at(turned(y, ky, Y), turned(x, kx, X), turned(core, kc, C))),

time: 30.5 us -> 30.1 us (0.987)
  Pallas kernels: 29.7 us -> 29.3 us
    pallas_call x1, Pallas kernels: 28.3 us -> 27.9 us  [local(): pl.pallas_call(functools.partial(kernel, count, chunks, factor), out_shap...]
where the time goes in v4:
time: 30.1 us; the launch traced here: 30 us
  Pallas kernels  29.3 us (97%)
  between operations  0.64 us (2%)
    pallas_call x1, Pallas kernels, local(): pl.pallas_call(functools.partial(kernel, count, chunks, factor), out_shap...  27.9 us
    pallas_call x1, Pallas kernels, local(): pl.pallas_call(finish, out_shape=(jax.ShapeDtypeStruct((rows, slab), F32)...  1.38 us

profile of v4, /device:TPU:1, one launch (start us, length us, event | category | flops | bytes accessed | tf_op | source)
XLA Modules:
  0.0 30.0 jit_solution(7986321346399561251)
XLA Ops:
  0.6 27.9 %shard_map.59 = (f32[64,384]{1,0:T(8,128)S(1)}, f32[64,384]{1,0:T(8,128)S(1)}, f32[64,384]{1,0:T(8,128)S(1)}, f32[64,384]{1,0:T(8,128)S(1)}, f32[64,384]{1,0:T(8...) custom-call(f32[896,384]{1,0:T(8,128)} %bitcast.3, ...), custom_call_target="tpu_custom_call" | custom-call | tf_op jit(solution)/shard_map/pallas_call | solution.py:285
  28.6 1.4 %shard_map.60 = (f32[896,384]{1,0:T(8,128)}, f32[8,384]{1,0:T(8,128)}) custom-call(f32[64,384]{1,0:T(8,128)S(1)} %get-tuple-element.34.refs_0_, f32[64,384]{1,0:T(8,128)S(1)} %get-tuple-element.35.refs_1_, f32[64,384]{1,0:T(8,128)S(1)} %get-tuple-element.36.refs_2_, f32[64,384]{1,0:T(8,128)S(1)} %get-tuple-element.37.refs_3_, ...), custom_call_target="tpu_custom_call" | custom-call | tf_op jit(solution)/shard_map/pallas_call | solution.py:316

commit v5 on v4

--- a/solution.py
+++ b/solution.py
@@ -49,7 +49,7 @@
 ):
     steps, images, rest = rest[:PIECES], rest[PIECES : 2 * PIECES], rest[2 * PIECES :]
     mix_ref, next_ref, w_v, h_v, g_v, start_v, parts_v, own, land, part = rest[:10]
-    first, second, load_sems, isend, irecv, sends, recvs = rest[10:]
+    first, second, load_sems, isend, irecv, sends, recvs, ready = rest[10:]
     tall_rows = steps[0].shape[0]
     r = lax.axis_index("blk")
     t = lax.axis_index("tp")
@@ -88,22 +88,19 @@
     def turned(v, k, size):
         return lax.rem(v + k, size)
 
-    peers = []
-    for kx in range(X):
-        for cc in range(C):
-            for side in (left, right):
-                peers.append((side, at(y, turned(x, kx, X), cc)))
+    sibling = (r, chip + 1 - core)
+    x_row = [(r, at(y, turned(x, k, X), core)) for k in range(1, X)]
+    y_column = [(r, at(turned(y, k, Y), x, core)) for k in range(1, Y)]
+    entry = [(right, t), (left, t), sibling] + x_row + y_column
     around = [(ky, kx, kc) for ky in range(Y) for kx in range(X) for kc in range(C)][1:]
     around.sort(key=lambda k: -min(k[0], Y - k[0]) - min(k[1], X - k[1]))
     along_x = sorted(range(X), key=lambda k: -min(k, X - k))
-    for ky, kx, kc in around:
-        peers.append((r, at(turned(y, ky, Y), turned(x, kx, X), turned(core, kc, C))))
-
-    def greet(some):
+
+    def greet(some, sem):
         for peer in some:
-            pl.semaphore_signal(barrier, inc=1, device_id=peer, device_id_type=MESH)
-
-    greet(peers[: 2 * X * C])
+            pl.semaphore_signal(sem, inc=1, device_id=peer, device_id_type=MESH)
+
+    greet(entry, barrier)
 
     part[...] = jnp.zeros_like(part)
     for copy in loads:
@@ -116,7 +113,6 @@
     grad_t = g_v[...].T
     felt = factor * folded(dot(tall, grad_t, ((1,), (0,))))
     felt_tall = jnp.concatenate(split3(felt), axis=0)
-    greet(peers[2 * X * C :])
 
     seen = []
     for i, (lo, size) in enumerate(chunks):
@@ -131,7 +127,8 @@
         own[0, :, span] = image[:RANK]
         own[1, :, span] = image[RANK:]
         if i == 0:
-            pl.semaphore_wait(barrier, len(peers))
+            pl.semaphore_wait(barrier, len(entry))
+            greet(x_row, ready.at[0])
         image_copies.append(
             (
                 send(own.at[0, :, span], land.at[1, :, span], isend.at[2 * i], irecv.at[2 * i], (right, t)),
@@ -148,6 +145,10 @@
         stacks = split3(stepped)
         for k in range(3):
             parts_v[k, span, :] = stacks[k]
+        if lo == 0:
+            pl.semaphore_wait(ready.at[0], len(x_row))
+            greet([sibling], ready.at[1])
+    pl.semaphore_wait(ready.at[1], 1)
 
     images_f = [[], []]
     for e in range(2):
@@ -308,6 +309,7 @@
             pltpu.SemaphoreType.DMA((2 * n,)),
             pltpu.SemaphoreType.DMA((2,)),
             pltpu.SemaphoreType.DMA((2,)),
+            pltpu.SemaphoreType.REGULAR((2,)),
         ],
         compiler_params=pltpu.CompilerParams(
             collective_id=0, has_side_effects=True, vmem_limit_bytes=53480 * 1024

time: 30.1 us -> 29 us (0.963)
  Pallas kernels: 29.3 us -> 28.2 us
    pallas_call x1, Pallas kernels: 27.9 us -> 26.8 us  [local(): pl.pallas_call(functools.partial(kernel, count, chunks, factor), out_shap...]
where the time goes in v5:
time: 29 us; the launch traced here: 28.8 us
  Pallas kernels  28.2 us (97%)
  between operations  0.64 us (2%)
    pallas_call x1, Pallas kernels, local(): pl.pallas_call(functools.partial(kernel, count, chunks, factor), out_shap...  26.8 us
    pallas_call x1, Pallas kernels, local(): pl.pallas_call(finish, out_shape=(jax.ShapeDtypeStruct((rows, slab), F32)...  1.38 us

profile of v5, /device:TPU:1, one launch (start us, length us, event | category | flops | bytes accessed | tf_op | source)
XLA Modules:
  0.0 28.8 jit_solution(15750866687492036397)
XLA Ops:
  0.6 26.8 %shard_map.59 = (f32[64,384]{1,0:T(8,128)S(1)}, f32[64,384]{1,0:T(8,128)S(1)}, f32[64,384]{1,0:T(8,128)S(1)}, f32[64,384]{1,0:T(8,128)S(1)}, f32[64,384]{1,0:T(8...) custom-call(f32[896,384]{1,0:T(8,128)} %bitcast.3, ...), custom_call_target="tpu_custom_call" | custom-call | tf_op jit(solution)/shard_map/pallas_call | solution.py:286
  27.4 1.4 %shard_map.60 = (f32[896,384]{1,0:T(8,128)}, f32[8,384]{1,0:T(8,128)}) custom-call(f32[64,384]{1,0:T(8,128)S(1)} %get-tuple-element.34.refs_0_, f32[64,384]{1,0:T(8,128)S(1)} %get-tuple-element.35.refs_1_, f32[64,384]{1,0:T(8,128)S(1)} %get-tuple-element.36.refs_2_, f32[64,384]{1,0:T(8,128)S(1)} %get-tuple-element.37.refs_3_, ...), custom_call_target="tpu_custom_call" | custom-call | tf_op jit(solution)/shard_map/pallas_call | solution.py:318

commit v6 on v5

--- a/solution.py
+++ b/solution.py
@@ -91,7 +91,7 @@
     sibling = (r, chip + 1 - core)
     x_row = [(r, at(y, turned(x, k, X), core)) for k in range(1, X)]
     y_column = [(r, at(turned(y, k, Y), x, core)) for k in range(1, Y)]
-    entry = [(right, t), (left, t), sibling] + x_row + y_column
+    entry = [(side, chip + cc) for side in (right, left) for cc in range(C)] + [sibling] + x_row + y_column
     around = [(ky, kx, kc) for ky in range(Y) for kx in range(X) for kc in range(C)][1:]
     around.sort(key=lambda k: -min(k[0], Y - k[0]) - min(k[1], X - k[1]))
     along_x = sorted(range(X), key=lambda k: -min(k, X - k))
@@ -145,10 +145,6 @@
         stacks = split3(stepped)
         for k in range(3):
             parts_v[k, span, :] = stacks[k]
-        if lo == 0:
-            pl.semaphore_wait(ready.at[0], len(x_row))
-            greet([sibling], ready.at[1])
-    pl.semaphore_wait(ready.at[1], 1)
 
     images_f = [[], []]
     for e in range(2):
@@ -171,25 +167,35 @@
         part[e, X - 1, :, :RANK] = 0.5 * gram
         aside = lax.rem(core + e, C)
         side, taker = ((right, 1), (left, 0))[e]
-        for kx in along_x:
-            tile = turned(x, kx, X)
-            send(
-                part.at[e, tile], first.at[X * C + C * ((-kx) % X) + core], sends.at[0], recvs.at[0],
-                (side, at(y, tile, taker)),
-            )
-        for kx in along_x:
-            tile = turned(x, kx, X)
-
-            def near():
+        if e == 0:
+            pl.semaphore_wait(ready.at[0], len(x_row))
+            greet([sibling], ready.at[1])
+
+        def across():
+            for kx in along_x:
+                tile = turned(x, kx, X)
                 send(
-                    part.at[e, tile], first.at[C * ((-kx) % X) + aside], sends.at[0], recvs.at[0],
-                    (r, at(y, tile, e)),
+                    part.at[e, tile], first.at[X * C + C * ((-kx) % X) + core], sends.at[0], recvs.at[0],
+                    (side, at(y, tile, taker)),
                 )
 
-            if kx:
-                near()
-            else:
-                pl.when(core != e)(near)
+        def within():
+            for kx in along_x:
+                tile = turned(x, kx, X)
+
+                def near():
+                    send(
+                        part.at[e, tile], first.at[C * ((-kx) % X) + aside], sends.at[0], recvs.at[0],
+                        (r, at(y, tile, e)),
+                    )
+
+                if kx:
+                    near()
+                else:
+                    pl.when(core != e)(near)
+
+        for step in (across, within) if e == 0 else (within, across):
+            step()
     first[0] = part[core, x]
     def whole(buf, step):
         return pltpu.make_async_remote_copy(
@@ -204,6 +210,7 @@
     while len(terms) > 1:
         terms = [a + b for a, b in zip(terms[::2], terms[1::2])]
     second[0] = terms[0]
+    pl.semaphore_wait(ready.at[1], 1)
     for ky, kx, kc in around:
         send(
             second.at[0], second.at[(((-ky) % Y) * X + (-kx) % X) * C + kc], sends.at[1], recvs.at[1],

time: 29 us -> 28.5 us (0.983)
  Pallas kernels: 28.2 us -> 27.7 us
    pallas_call x1, Pallas kernels: 26.8 us -> 26.3 us  [local(): pl.pallas_call(functools.partial(kernel, count, chunks, factor), out_shap...]
where the time goes in v6:
time: 28.5 us; the launch traced here: 28.4 us
  Pallas kernels  27.7 us (97%)
  between operations  0.64 us (2%)
    pallas_call x1, Pallas kernels, local(): pl.pallas_call(functools.partial(kernel, count, chunks, factor), out_shap...  26.3 us
    pallas_call x1, Pallas kernels, local(): pl.pallas_call(finish, out_shape=(jax.ShapeDtypeStruct((rows, slab), F32)...  1.38 us

profile of v6, /device:TPU:1, one launch (start us, length us, event | category | flops | bytes accessed | tf_op | source)
XLA Modules:
  0.0 28.4 jit_solution(7086121494156012260)
XLA Ops:
  0.6 26.3 %shard_map.59 = (f32[64,384]{1,0:T(8,128)S(1)}, f32[64,384]{1,0:T(8,128)S(1)}, f32[64,384]{1,0:T(8,128)S(1)}, f32[64,384]{1,0:T(8,128)S(1)}, f32[64,384]{1,0:T(8...) custom-call(f32[896,384]{1,0:T(8,128)} %bitcast.3, ...), custom_call_target="tpu_custom_call" | custom-call | tf_op jit(solution)/shard_map/pallas_call | solution.py:293
  27.0 1.4 %shard_map.60 = (f32[896,384]{1,0:T(8,128)}, f32[8,384]{1,0:T(8,128)}) custom-call(f32[64,384]{1,0:T(8,128)S(1)} %get-tuple-element.34.refs_0_, f32[64,384]{1,0:T(8,128)S(1)} %get-tuple-element.35.refs_1_, f32[64,384]{1,0:T(8,128)S(1)} %get-tuple-element.36.refs_2_, f32[64,384]{1,0:T(8,128)S(1)} %get-tuple-element.37.refs_3_, ...), custom_call_target="tpu_custom_call" | custom-call | tf_op jit(solution)/shard_map/pallas_call | solution.py:325

commit v7 on v6

--- a/solution.py
+++ b/solution.py
@@ -67,10 +67,10 @@
     loads = [
         pltpu.make_async_copy(s_hbm.at[r], start_v.at[0], load_sems.at[1]),
         pltpu.make_async_copy(s_hbm.at[left], start_v.at[1], load_sems.at[2]),
-        pltpu.make_async_copy(g_hbm, g_v, load_sems.at[0]),
     ]
     for copy in loads:
         copy.start()
+    g_load = pltpu.make_async_copy(g_hbm, g_v, load_sems.at[0])
     chunk_loads = []
     for i, (lo, size) in enumerate(chunks):
         w_copy = pltpu.make_async_copy(
@@ -81,6 +81,7 @@
         )
         w_copy.start()
         chunk_loads.append((w_copy, h_copy))
+    g_load.start()
     for pair in chunk_loads:
         pair[1].start()
 
@@ -110,15 +111,15 @@
     tall = jnp.concatenate(start_parts, axis=0)
     n = 2 * RANK
     tall_t = tall.T
-    grad_t = g_v[...].T
-    felt = factor * folded(dot(tall, grad_t, ((1,), (0,))))
-    felt_tall = jnp.concatenate(split3(felt), axis=0)
 
     seen = []
     for i, (lo, size) in enumerate(chunks):
         chunk_loads[i][0].wait()
         high, mid, low = [dot(v, tall_t, ((1,), (0,))) for v in split3(w_v[pl.ds(lo, size), :])]
         seen.append(folded((high + (mid + low)).T))
+    g_load.wait()
+    felt = factor * folded(dot(g_v[...], tall_t, ((1,), (0,))).T)
+    felt_tall = jnp.concatenate(split3(felt), axis=0)
     image_copies = []
     for i, (lo, size) in enumerate(chunks):
         span = pl.ds(lo, size)
@@ -138,8 +139,8 @@
 
     for lo, size in chunks:
         span = pl.ds(lo, size)
-        gradient = dot(grad_t, h_v[:, span], ((1,), (0,)))
-        stepped = w_v[span, :] - factor * gradient.T
+        gradient = dot(h_v[:, span], g_v[...], ((0,), (0,)))
+        stepped = w_v[span, :] - factor * gradient
         for p in range(lo // tall_rows, (lo + size) // tall_rows):
             steps[p][...] = stepped[p * tall_rows - lo : (p + 1) * tall_rows - lo]
         stacks = split3(stepped)

time: 28.5 us -> 28.6 us (level)
  no operation moved by 1% of the time
where the time goes in v7:
time: 28.6 us; the launch traced here: 28.4 us
  Pallas kernels  27.8 us (97%)
  between operations  0.64 us (2%)
    pallas_call x1, Pallas kernels, local(): pl.pallas_call(functools.partial(kernel, count, chunks, factor), out_shap...  26.4 us
    pallas_call x1, Pallas kernels, local(): pl.pallas_call(finish, out_shape=(jax.ShapeDtypeStruct((rows, slab), F32)...  1.38 us

profile of v7, /device:TPU:1, one launch (start us, length us, event | category | flops | bytes accessed | tf_op | source)
XLA Modules:
  0.0 28.4 jit_solution(444027712494547312)
XLA Ops:
  0.6 26.4 %shard_map.59 = (f32[64,384]{1,0:T(8,128)S(1)}, f32[64,384]{1,0:T(8,128)S(1)}, f32[64,384]{1,0:T(8,128)S(1)}, f32[64,384]{1,0:T(8,128)S(1)}, f32[64,384]{1,0:T(8...) custom-call(f32[896,384]{1,0:T(8,128)} %bitcast.3, ...), custom_call_target="tpu_custom_call" | custom-call | tf_op jit(solution)/shard_map/pallas_call | solution.py:294
  27.0 1.4 %shard_map.60 = (f32[896,384]{1,0:T(8,128)}, f32[8,384]{1,0:T(8,128)}) custom-call(f32[64,384]{1,0:T(8,128)S(1)} %get-tuple-element.34.refs_0_, f32[64,384]{1,0:T(8,128)S(1)} %get-tuple-element.35.refs_1_, f32[64,384]{1,0:T(8,128)S(1)} %get-tuple-element.36.refs_2_, f32[64,384]{1,0:T(8,128)S(1)} %get-tuple-element.37.refs_3_, ...), custom_call_target="tpu_custom_call" | custom-call | tf_op jit(solution)/shard_map/pallas_call | solution.py:326

commit v8 on v7

--- a/solution.py
+++ b/solution.py
@@ -64,6 +64,23 @@
     def at(yy, xx, cc):
         return (yy * X + xx) * C + cc
 
+    barrier = pltpu.get_barrier_semaphore()
+    def turned(v, k, size):
+        return lax.rem(v + k, size)
+
+    sibling = (r, chip + 1 - core)
+    x_row = [(r, at(y, turned(x, k, X), core)) for k in range(1, X)]
+    y_column = [(r, at(turned(y, k, Y), x, core)) for k in range(1, Y)]
+    entry = [(side, chip + cc) for side in (right, left) for cc in range(C)] + [sibling] + x_row + y_column
+    around = [(ky, kx, kc) for ky in range(Y) for kx in range(X) for kc in range(C)][1:]
+    around.sort(key=lambda k: -min(k[0], Y - k[0]) - min(k[1], X - k[1]))
+    along_x = sorted(range(X), key=lambda k: -min(k, X - k))
+
+    def greet(some, sem):
+        for peer in some:
+            pl.semaphore_signal(sem, inc=1, device_id=peer, device_id_type=MESH)
+
+    greet(entry[: 2 * C], barrier)
     loads = [
         pltpu.make_async_copy(s_hbm.at[r], start_v.at[0], load_sems.at[1]),
         pltpu.make_async_copy(s_hbm.at[left], start_v.at[1], load_sems.at[2]),
@@ -85,23 +102,7 @@
     for pair in chunk_loads:
         pair[1].start()
 
-    barrier = pltpu.get_barrier_semaphore()
-    def turned(v, k, size):
-        return lax.rem(v + k, size)
-
-    sibling = (r, chip + 1 - core)
-    x_row = [(r, at(y, turned(x, k, X), core)) for k in range(1, X)]
-    y_column = [(r, at(turned(y, k, Y), x, core)) for k in range(1, Y)]
-    entry = [(side, chip + cc) for side in (right, left) for cc in range(C)] + [sibling] + x_row + y_column
-    around = [(ky, kx, kc) for ky in range(Y) for kx in range(X) for kc in range(C)][1:]
-    around.sort(key=lambda k: -min(k[0], Y - k[0]) - min(k[1], X - k[1]))
-    along_x = sorted(range(X), key=lambda k: -min(k, X - k))
-
-    def greet(some, sem):
-        for peer in some:
-            pl.semaphore_signal(sem, inc=1, device_id=peer, device_id_type=MESH)
-
-    greet(entry, barrier)
+    greet(entry[2 * C :], barrier)
 
     part[...] = jnp.zeros_like(part)
     for copy in loads:
@@ -129,13 +130,14 @@
         own[1, :, span] = image[RANK:]
         if i == 0:
             pl.semaphore_wait(barrier, len(entry))
-            greet(x_row, ready.at[0])
         image_copies.append(
             (
                 send(own.at[0, :, span], land.at[1, :, span], isend.at[2 * i], irecv.at[2 * i], (right, t)),
                 send(own.at[1, :, span], land.at[0, :, span], isend.at[2 * i + 1], irecv.at[2 * i + 1], (left, t)),
             )
         )
+        if i == 0:
+            greet(x_row, ready.at[0])
 
     for lo, size in chunks:
         span = pl.ds(lo, size)
@@ -150,7 +152,7 @@
     images_f = [[], []]
     for e in range(2):
         product = jnp.zeros((3 * RANK, slab), F32)
-        gram = jnp.zeros((3 * RANK, RANK), F32)
+        gram = jnp.zeros((3 * RANK, 3 * RANK), F32)
         for i, (lo, size) in enumerate(chunks):
             span = pl.ds(lo, size)
             image_copies[i][1 - e].wait_recv()
@@ -158,13 +160,14 @@
             images_f[e].append(image)
             pieces = split3(image)
             rows = jnp.concatenate([v.astype(F32) for v in pieces], axis=0).astype(BF16)
+            gram = gram + dot(rows, rows, ((1,), (1,)))
             for k in range(3):
                 product = product + dot(rows, parts_v[k, span, :], ((1,), (0,)))
-                gram = gram + dot(rows, pieces[k], ((1,), (1,)))
         product, gram = folded(product), folded(gram)
         for k in range(X - 1):
             block = product[:, 128 * k : 128 * (k + 1)]
             part[e, k] = block if e == 0 else -block
+        gram = gram[:, :RANK] + (gram[:, RANK : 2 * RANK] + gram[:, 2 * RANK :])
         part[e, X - 1, :, :RANK] = 0.5 * gram
         aside = lax.rem(core + e, C)
         side, taker = ((right, 1), (left, 0))[e]

time: 28.6 us -> 28.6 us (level)
  no operation moved by 1% of the time
where the time goes in v8:
time: 28.6 us; the launch traced here: 28.5 us
  Pallas kernels  27.8 us (97%)
  between operations  0.64 us (2%)
    pallas_call x1, Pallas kernels, local(): pl.pallas_call(functools.partial(kernel, count, chunks, factor), out_shap...  26.4 us
    pallas_call x1, Pallas kernels, local(): pl.pallas_call(finish, out_shape=(jax.ShapeDtypeStruct((rows, slab), F32)...  1.38 us

profile of v8, /device:TPU:1, one launch (start us, length us, event | category | flops | bytes accessed | tf_op | source)
XLA Modules:
  0.0 28.5 jit_solution(18059627649016430017)
XLA Ops:
  0.6 26.4 %shard_map.59 = (f32[64,384]{1,0:T(8,128)S(1)}, f32[64,384]{1,0:T(8,128)S(1)}, f32[64,384]{1,0:T(8,128)S(1)}, f32[64,384]{1,0:T(8,128)S(1)}, f32[64,384]{1,0:T(8...) custom-call(f32[896,384]{1,0:T(8,128)} %bitcast.3, ...), custom_call_target="tpu_custom_call" | custom-call | tf_op jit(solution)/shard_map/pallas_call | solution.py:297
  27.1 1.4 %shard_map.60 = (f32[896,384]{1,0:T(8,128)}, f32[8,384]{1,0:T(8,128)}) custom-call(f32[64,384]{1,0:T(8,128)S(1)} %get-tuple-element.34.refs_0_, f32[64,384]{1,0:T(8,128)S(1)} %get-tuple-element.35.refs_1_, f32[64,384]{1,0:T(8,128)S(1)} %get-tuple-element.36.refs_2_, f32[64,384]{1,0:T(8,128)S(1)} %get-tuple-element.37.refs_3_, ...), custom_call_target="tpu_custom_call" | custom-call | tf_op jit(solution)/shard_map/pallas_call | solution.py:329

commit v9 on v7

--- a/solution.py
+++ b/solution.py
@@ -286,7 +286,7 @@
     _, rows, slab = weights.shape
     tokens = hidden.shape[0]
     factor = step_rate / math.sqrt(tokens)
-    chunks = [(0, 512), (512, rows - 512)]
+    chunks = [(0, 640), (640, rows - 640)]
     n = len(chunks)
     terms = 12 * RANK
     in_vmem = pl.BlockSpec(memory_space=pltpu.VMEM)

time: 28.6 us -> 28.7 us (level)
  no operation moved by 1% of the time
where the time goes in v9:
time: 28.7 us; the launch traced here: 28.5 us
  Pallas kernels  27.9 us (97%)
  between operations  0.64 us (2%)
    pallas_call x1, Pallas kernels, local(): pl.pallas_call(functools.partial(kernel, count, chunks, factor), out_shap...  26.5 us
    pallas_call x1, Pallas kernels, local(): pl.pallas_call(finish, out_shape=(jax.ShapeDtypeStruct((rows, slab), F32)...  1.38 us

profile of v9, /device:TPU:1, one launch (start us, length us, event | category | flops | bytes accessed | tf_op | source)
XLA Modules:
  0.0 28.5 jit_solution(8636212022542925822)
XLA Ops:
  0.6 26.5 %shard_map.59 = (f32[64,384]{1,0:T(8,128)S(1)}, f32[64,384]{1,0:T(8,128)S(1)}, f32[64,384]{1,0:T(8,128)S(1)}, f32[64,384]{1,0:T(8,128)S(1)}, f32[64,384]{1,0:T(8...) custom-call(f32[896,384]{1,0:T(8,128)} %bitcast.3, ...), custom_call_target="tpu_custom_call" | custom-call | tf_op jit(solution)/shard_map/pallas_call | solution.py:294
  27.1 1.4 %shard_map.60 = (f32[896,384]{1,0:T(8,128)}, f32[8,384]{1,0:T(8,128)}) custom-call(f32[64,384]{1,0:T(8,128)S(1)} %get-tuple-element.34.refs_0_, f32[64,384]{1,0:T(8,128)S(1)} %get-tuple-element.35.refs_1_, f32[64,384]{1,0:T(8,128)S(1)} %get-tuple-element.36.refs_2_, f32[64,384]{1,0:T(8,128)S(1)} %get-tuple-element.37.refs_3_, ...), custom_call_target="tpu_custom_call" | custom-call | tf_op jit(solution)/shard_map/pallas_call | solution.py:326

commit v10 on v7

--- a/solution.py
+++ b/solution.py
@@ -150,7 +150,7 @@
     images_f = [[], []]
     for e in range(2):
         product = jnp.zeros((3 * RANK, slab), F32)
-        gram = jnp.zeros((3 * RANK, RANK), F32)
+        gram = jnp.zeros((3 * RANK, 3 * RANK), F32)
         for i, (lo, size) in enumerate(chunks):
             span = pl.ds(lo, size)
             image_copies[i][1 - e].wait_recv()
@@ -158,13 +158,14 @@
             images_f[e].append(image)
             pieces = split3(image)
             rows = jnp.concatenate([v.astype(F32) for v in pieces], axis=0).astype(BF16)
+            gram = gram + dot(rows, rows, ((1,), (1,)))
             for k in range(3):
                 product = product + dot(rows, parts_v[k, span, :], ((1,), (0,)))
-                gram = gram + dot(rows, pieces[k], ((1,), (1,)))
         product, gram = folded(product), folded(gram)
         for k in range(X - 1):
             block = product[:, 128 * k : 128 * (k + 1)]
             part[e, k] = block if e == 0 else -block
+        gram = gram[:, :RANK] + (gram[:, RANK : 2 * RANK] + gram[:, 2 * RANK :])
         part[e, X - 1, :, :RANK] = 0.5 * gram
         aside = lax.rem(core + e, C)
         side, taker = ((right, 1), (left, 0))[e]

time: 28.6 us -> 28.6 us (level)
  no operation moved by 1% of the time
where the time goes in v10:
time: 28.6 us; the launch traced here: 28.4 us
  Pallas kernels  27.8 us (97%)
  between operations  0.64 us (2%)
    pallas_call x1, Pallas kernels, local(): pl.pallas_call(functools.partial(kernel, count, chunks, factor), out_shap...  26.4 us
    pallas_call x1, Pallas kernels, local(): pl.pallas_call(finish, out_shape=(jax.ShapeDtypeStruct((rows, slab), F32)...  1.38 us

profile of v10, /device:TPU:1, one launch (start us, length us, event | category | flops | bytes accessed | tf_op | source)
XLA Modules:
  0.0 28.4 jit_solution(12466727609999483455)
XLA Ops:
  0.6 26.4 %shard_map.59 = (f32[64,384]{1,0:T(8,128)S(1)}, f32[64,384]{1,0:T(8,128)S(1)}, f32[64,384]{1,0:T(8,128)S(1)}, f32[64,384]{1,0:T(8,128)S(1)}, f32[64,384]{1,0:T(8...) custom-call(f32[896,384]{1,0:T(8,128)} %bitcast.3, ...), custom_call_target="tpu_custom_call" | custom-call | tf_op jit(solution)/shard_map/pallas_call | solution.py:295
  27.1 1.4 %shard_map.60 = (f32[896,384]{1,0:T(8,128)}, f32[8,384]{1,0:T(8,128)}) custom-call(f32[64,384]{1,0:T(8,128)S(1)} %get-tuple-element.34.refs_0_, f32[64,384]{1,0:T(8,128)S(1)} %get-tuple-element.35.refs_1_, f32[64,384]{1,0:T(8,128)S(1)} %get-tuple-element.36.refs_2_, f32[64,384]{1,0:T(8,128)S(1)} %get-tuple-element.37.refs_3_, ...), custom_call_target="tpu_custom_call" | custom-call | tf_op jit(solution)/shard_map/pallas_call | solution.py:327
